TPU v7x, 32 devices: a whole 2x2x4 slice. The times are simulated.
32 devices in a mesh: dp: 16 (over z, y, x), feat: 2 (over core).
Axes of the slice: x: 2, y: 2, z: 4, core: 2. Of those that a mesh axis runs over, the one named last changes fastest.
Arguments:
- inputs: float32 [20480, 640], P('dp', 'feat'), may hold values from -6 to 6
- encoder: bfloat16 [20480, 640], P('dp', 'feat'), may hold values from -6 to 6
- output_grad: float32 [20480, 640], P('dp', 'feat'), may hold values from -6 to 6
- target_lengths: int32 [32, 24], P(('dp', 'feat')), may hold values from 0 to 256, as said below
- source_lengths: int32 [32, 24], P(('dp', 'feat')), may hold values from 0 to 256, as said below
- gains: float32 [3, 640], P(None, 'feat'), may hold values from 0.5 to 1.5
- shifts: float32 [3, 640], P(None, 'feat'), may hold values from -2 to 2
- self_inproj: bfloat16 [640, 1920], replicated, may hold values from -0.25 to 0.25
- self_outproj: bfloat16 [640, 640], replicated, may hold values from -1 to 1
- cross_query: bfloat16 [640, 640], replicated, may hold values from -0.25 to 0.25
- cross_keyvalue: bfloat16 [640, 1280], replicated, may hold values from -0.25 to 0.25
- cross_outproj: bfloat16 [640, 640], replicated, may hold values from -1 to 1
- ffn_expand: bfloat16 [640, 3072], replicated, may hold values from -0.25 to 0.25
- ffn_reduce: bfloat16 [3072, 640], replicated, may hold values from -0.109375 to 0.109375
Outputs:
- layer_out: float32 [20480, 640], P('dp', 'feat')
- input_grad: float32 [20480, 640], P('dp', 'feat')
- encoder_grad: float32 [20480, 640], P('dp', 'feat')
- gain_grad: float32 [3, 640], P(None, 'feat')
- shift_grad: float32 [3, 640], P(None, 'feat')
- self_inproj_grad: float32 [640, 1920], P('dp', 'feat')
- self_outproj_grad: float32 [640, 640], P('dp', 'feat')
- cross_query_grad: float32 [640, 640], P('dp', 'feat')
- cross_keyvalue_grad: float32 [640, 1280], P('dp', 'feat')
- cross_outproj_grad: float32 [640, 640], P('dp', 'feat')
- ffn_expand_grad: float32 [640, 3072], P('dp', 'feat')
- ffn_reduce_grad: float32 [3072, 640], P('dp', 'feat')
Inputs may be any that keep to these rules, and one draw needn't show every extreme that they name: `target_lengths`: in each bucket the nonzero lengths fill the first slots and zeros the rest; a bucket's lengths sum to 640 or less; in every draw one bucket, chosen from the seed, has a first sentence of 256. `source_lengths`: nonzero exactly where target_lengths is, and at most the target length.
All inputs are finite; a program needn't handle non-finite values.
Results may differ from a plain program's by a relative error of at most 0.017.
Values may be sent and summed in bfloat16 or wider, within the bound.
A program may use at most 192 MiB of HBM per device.

v0:
```python
import math
import jax
import jax.numpy as jnp
from jax import lax
from jax.sharding import PartitionSpec as P

HEADS = 8
EPSILON = 1e-05
MASKED_SCORE = -1e30


def as_sent(array):

    def short(part):
        return part.astype(jnp.bfloat16) if part.dtype == jnp.float32 else part

    return jax.tree.map(short, array)


def inner(left, right):
    return lax.dot_general(
        left, right, (((0,), (0,)), ((), ())), preferred_element_type=jnp.float32
    )


def backward_product(grad, weight):
    return lax.dot_general(
        grad, weight, (((1,), (1,)), ((), ())), preferred_element_type=jnp.float32
    )


def smooth_gate(values):
    return jax.nn.gelu(values, approximate=True)


def row_sums(first, second):
    return (first, second)


def to_tokens(parts):
    return parts


def to_features(parts):
    return parts


def gather_rows(part):
    return lax.all_to_all(part, "feat", split_axis=0, concat_axis=1, tiled=True)


def spread_rows(part):
    return lax.all_to_all(part, "feat", split_axis=1, concat_axis=0, tiled=True)


def norm_forward(values, gain, shift):
    width = values.shape[1]
    total, squares = row_sums(jnp.sum(values, axis=1), jnp.sum(values * values, axis=1))
    center = total / width
    reciprocal = lax.rsqrt(squares / width - center * center + EPSILON)
    normed = (values - center[:, None]) * reciprocal[:, None]
    return (normed, reciprocal, (normed * gain + shift).astype(jnp.bfloat16))


def norm_backward(grad_normed, normed, reciprocal, gain):
    width = normed.shape[1]
    grad_value = grad_normed.astype(jnp.float32)
    scaled = grad_value * gain
    first, second = row_sums(jnp.sum(scaled, axis=1), jnp.sum(scaled * normed, axis=1))
    grad_input = reciprocal[:, None] * (
        scaled - first[:, None] / width - normed * (second[:, None] / width)
    )
    return (grad_input, jnp.sum(grad_value * normed, axis=0), jnp.sum(grad_value, axis=0))


def sentence_rows(lengths, count):
    slots = jnp.arange(lengths.shape[1], dtype=jnp.int32)
    ends = jnp.sum(
        jnp.where(slots[:, None] <= slots[None, :], lengths[0][:, None], 0), axis=0, dtype=jnp.int32
    )
    positions = jnp.arange(count, dtype=jnp.int32)
    sentence = jnp.sum(
        (ends[None, :] <= positions[:, None]).astype(jnp.int32), axis=1, dtype=jnp.int32
    )
    return (sentence, positions < ends[-1])


def split_heads(values):
    return values.reshape(values.shape[0], HEADS, values.shape[1] // HEADS)


def head_scores(queries, keys, allowed):
    head_size = queries.shape[1] // HEADS
    scores = jnp.einsum(
        "qhd,khd->hqk", split_heads(queries), split_heads(keys), preferred_element_type=jnp.float32
    ) * (1.0 / math.sqrt(head_size))
    return jnp.where(allowed[None, :, :], scores, MASKED_SCORE)


def attend_forward(queries, keys, values, allowed):
    scores = head_scores(queries, keys, allowed)
    largest = jnp.max(scores, axis=-1, keepdims=True)
    expo = jnp.exp(scores - largest)
    total = jnp.sum(expo, axis=-1, keepdims=True)
    weights = expo / total
    mixed = jnp.einsum(
        "hqk,khd->qhd",
        weights.astype(jnp.bfloat16),
        split_heads(values),
        preferred_element_type=jnp.float32,
    )
    log_total = largest[..., 0] + jnp.log(total[..., 0])
    return (mixed.reshape(queries.shape).astype(jnp.bfloat16), log_total)


def attend_backward(queries, keys, values, allowed, log_total, grad_mixed):
    head_size = queries.shape[1] // HEADS
    scale = 1.0 / math.sqrt(head_size)
    weights = jnp.exp(head_scores(queries, keys, allowed) - log_total[..., None])
    grad_heads = split_heads(grad_mixed)
    grad_weights = jnp.einsum(
        "qhd,khd->hqk", grad_heads, split_heads(values), preferred_element_type=jnp.float32
    )
    grad_values = jnp.einsum(
        "hqk,qhd->khd", weights.astype(jnp.bfloat16), grad_heads, preferred_element_type=jnp.float32
    )
    centre = jnp.sum(weights * grad_weights, axis=-1, keepdims=True)
    grad_scores = (weights * (grad_weights - centre)).astype(jnp.bfloat16)
    grad_queries = (
        jnp.einsum(
            "hqk,khd->qhd", grad_scores, split_heads(keys), preferred_element_type=jnp.float32
        )
        * scale
    )
    grad_keys = (
        jnp.einsum(
            "hqk,qhd->khd", grad_scores, split_heads(queries), preferred_element_type=jnp.float32
        )
        * scale
    )
    return (
        grad_queries.reshape(queries.shape),
        grad_keys.reshape(keys.shape),
        grad_values.reshape(values.shape),
    )


def masked_rows(grad, valid):
    return jnp.where(valid[:, None], grad, jnp.zeros_like(grad))


def per_device(
    inputs,
    encoder,
    output_grad,
    target_lengths,
    source_lengths,
    gains,
    shifts,
    self_inproj,
    self_outproj,
    cross_query,
    cross_keyvalue,
    cross_outproj,
    ffn_expand,
    ffn_reduce,
):
    inputs = gather_rows(inputs)
    encoder = gather_rows(encoder)
    output_grad = gather_rows(output_grad)
    gains = lax.all_gather(gains, "feat", axis=1, tiled=True)
    shifts = lax.all_gather(shifts, "feat", axis=1, tiled=True)
    count = inputs.shape[0]
    width = self_outproj.shape[0]
    target_seg, target_valid = sentence_rows(target_lengths, count)
    source_seg, source_valid = sentence_rows(source_lengths, count)
    positions = jnp.arange(count, dtype=jnp.int32)
    keep = target_valid.astype(jnp.float32)[:, None]
    self_mask = (target_seg[:, None] == target_seg[None, :]) & (
        positions[None, :] <= positions[:, None]
    )
    self_mask = self_mask & target_valid[:, None] & target_valid[None, :]
    cross_mask = (
        (target_seg[:, None] == source_seg[None, :]) & target_valid[:, None] & source_valid[None, :]
    )
    normed_one, recip_one, normed_cols = norm_forward(inputs, gains[0], shifts[0])
    (normed1,) = to_tokens((normed_cols,))
    projected = jnp.dot(normed1, self_inproj, preferred_element_type=jnp.float32).astype(
        jnp.bfloat16
    )
    queries = projected[:, :width]
    keys = projected[:, width : 2 * width]
    values = projected[:, 2 * width :]
    attended1, log_one = attend_forward(queries, keys, values, self_mask)
    branch = (jnp.dot(attended1, self_outproj, preferred_element_type=jnp.float32) * keep).astype(
        jnp.bfloat16
    )
    (branch_cols,) = to_features((branch,))
    mid_one = inputs + branch_cols.astype(jnp.float32)
    normed_two, recip_two, normed_cols = norm_forward(mid_one, gains[1], shifts[1])
    normed2, source_rows = to_tokens((normed_cols, encoder))
    cross_queries = jnp.dot(normed2, cross_query, preferred_element_type=jnp.float32).astype(
        jnp.bfloat16
    )
    memory = jnp.dot(source_rows, cross_keyvalue, preferred_element_type=jnp.float32).astype(
        jnp.bfloat16
    )
    attended2, log_two = attend_forward(
        cross_queries, memory[:, :width], memory[:, width:], cross_mask
    )
    branch = (jnp.dot(attended2, cross_outproj, preferred_element_type=jnp.float32) * keep).astype(
        jnp.bfloat16
    )
    (branch_cols,) = to_features((branch,))
    mid_two = mid_one + branch_cols.astype(jnp.float32)
    normed_three, recip_three, normed_cols = norm_forward(mid_two, gains[2], shifts[2])
    (normed3,) = to_tokens((normed_cols,))
    expanded = jnp.dot(normed3, ffn_expand, preferred_element_type=jnp.float32).astype(jnp.bfloat16)
    gated, gate_pull = jax.vjp(smooth_gate, expanded.astype(jnp.float32))
    activated = gated.astype(jnp.bfloat16)
    branch = (jnp.dot(activated, ffn_reduce, preferred_element_type=jnp.float32) * keep).astype(
        jnp.bfloat16
    )
    (branch_cols,) = to_features((branch,))
    layer_out = mid_two + branch_cols.astype(jnp.float32)
    (grad_branch,) = to_tokens((output_grad.astype(jnp.bfloat16),))
    grad_branch = masked_rows(grad_branch, target_valid)
    reduce_grad = inner(activated, grad_branch)
    grad_act = backward_product(grad_branch, ffn_reduce)
    (grad_pre,) = gate_pull(grad_act)
    grad_expanded = grad_pre.astype(jnp.bfloat16)
    expand_grad = inner(normed3, grad_expanded)
    grad_normed = backward_product(grad_expanded, ffn_expand).astype(jnp.bfloat16)
    (grad_cols,) = to_features((grad_normed,))
    part_three, gain_three, shift_three = norm_backward(
        grad_cols, normed_three, recip_three, gains[2]
    )
    grad_mid_two = output_grad + part_three
    (grad_branch,) = to_tokens((grad_mid_two.astype(jnp.bfloat16),))
    grad_branch = masked_rows(grad_branch, target_valid)
    cross_out_grad = inner(attended2, grad_branch)
    grad_attended = backward_product(grad_branch, cross_outproj).astype(jnp.bfloat16)
    grad_cq, grad_ck, grad_cv = attend_backward(
        cross_queries, memory[:, :width], memory[:, width:], cross_mask, log_two, grad_attended
    )
    grad_cq = grad_cq.astype(jnp.bfloat16)
    grad_memory = jnp.concatenate([grad_ck, grad_cv], axis=1).astype(jnp.bfloat16)
    cross_query_grad = inner(normed2, grad_cq)
    cross_kv_grad = inner(source_rows, grad_memory)
    grad_normed = backward_product(grad_cq, cross_query).astype(jnp.bfloat16)
    grad_source = backward_product(grad_memory, cross_keyvalue).astype(jnp.bfloat16)
    grad_cols, grad_source_cols = to_features((grad_normed, grad_source))
    part_two, gain_two, shift_two = norm_backward(grad_cols, normed_two, recip_two, gains[1])
    grad_mid_one = grad_mid_two + part_two
    (grad_branch,) = to_tokens((grad_mid_one.astype(jnp.bfloat16),))
    grad_branch = masked_rows(grad_branch, target_valid)
    self_out_grad = inner(attended1, grad_branch)
    grad_attended = backward_product(grad_branch, self_outproj).astype(jnp.bfloat16)
    grad_q, grad_k, grad_v = attend_backward(
        queries, keys, values, self_mask, log_one, grad_attended
    )
    grad_projected = jnp.concatenate([grad_q, grad_k, grad_v], axis=1).astype(jnp.bfloat16)
    self_in_grad = inner(normed1, grad_projected)
    grad_normed = backward_product(grad_projected, self_inproj).astype(jnp.bfloat16)
    (grad_cols,) = to_features((grad_normed,))
    part_one, gain_one, shift_one = norm_backward(grad_cols, normed_one, recip_one, gains[0])
    input_grad = grad_mid_one + part_one
    gain_local = jnp.stack([gain_one, gain_two, gain_three], axis=0)
    shift_local = jnp.stack([shift_one, shift_two, shift_three], axis=0)
    vectors = lax.psum(jnp.concatenate([gain_local, shift_local], axis=0), ("dp", "feat"))
    half = vectors.shape[1] // lax.axis_size("feat")
    vectors = lax.dynamic_slice_in_dim(vectors, lax.axis_index("feat") * half, half, axis=1)
    gain_grad, shift_grad = (vectors[:3], vectors[3:])
    weight_terms = (
        self_in_grad,
        self_out_grad,
        cross_query_grad,
        cross_kv_grad,
        cross_out_grad,
        expand_grad,
        reduce_grad,
    )
    summed = []
    for term in weight_terms:
        pair = lax.psum_scatter(term.astype(jnp.bfloat16), "feat", scatter_dimension=1, tiled=True)
        summed.append(
            lax.psum_scatter(pair, "dp", scatter_dimension=0, tiled=True).astype(jnp.float32)
        )
    return (
        spread_rows(layer_out),
        spread_rows(input_grad),
        spread_rows(grad_source_cols).astype(jnp.float32),
        gain_grad,
        shift_grad,
        *summed,
    )


def solution(mesh):
    in_specs = (
        P("dp", "feat"),
        P("dp", "feat"),
        P("dp", "feat"),
        P(("dp", "feat"), None),
        P(("dp", "feat"), None),
        P(None, "feat"),
        P(None, "feat"),
        P(),
        P(),
        P(),
        P(),
        P(),
        P(),
        P(),
    )
    out_specs = (
        P("dp", "feat"),
        P("dp", "feat"),
        P("dp", "feat"),
        P(None, "feat"),
        P(None, "feat"),
        P("dp", "feat"),
        P("dp", "feat"),
        P("dp", "feat"),
        P("dp", "feat"),
        P("dp", "feat"),
        P("dp", "feat"),
        P("dp", "feat"),
    )
    return jax.shard_map(
        per_device, mesh=mesh, in_specs=in_specs, out_specs=out_specs, check_vma=False
    )
```

profile of v0, /device:TPU:0, one launch (start us, length us, event | category | flops | bytes accessed | tf_op | source)
XLA Modules:
  0.0 732.3 jit_solution(13034640641992369800)
XLA Ops:
  7.2 2.3 copy.193
  9.5 3.5 all-to-all-start.1
  16.5 2.0 all-gather
  18.6 1.8 all-gather.1
  20.5 2.7 copy.192
  23.2 4.7 all-to-all-start
  27.8 2.9 convolution_convert_fusion.6
  31.8 2.2 copy.144
  35.3 2.7 copy.191
  38.0 4.7 all-to-all-start.3
  46.0 1.7 add_convert_fusion.2
  47.7 2.2 convolution_convert_fusion.4
  51.4 2.2 copy.140
  53.6 2.2 copy.139
  58.6 8.8 %fusion.79 = f32[640,3072]{1,0:T(8,128)} fusion(bf16[640,640]{0,1:T(8,128)(2,1)S(1)} %fusion.60, bf16[3072,640]{1,0:T(8,128)(2,1)} %param.27), kind=kOutput, calls=%fused_computation.178 | convolution fusion | flops 2516582400 | bytes 12615680 | tf_op jit(solution)/shard_map/dot_general | solution.py:27
  68.6 2.5 fusion.77
  71.1 1.7 fusion
  72.9 2.9 copy-done.1
  75.8 3.7 fusion.59
  79.5 2.8 fusion.73
  84.1 2.5 fusion.78
  86.7 2.0 fusion.1
  88.7 2.7 copy-done.2
  91.4 3.8 fusion.58
  97.4 12.5 %fusion.7 = (bf16[640,3072]{1,0:T(8,128)(2,1)S(1)}, bf16[640,3072]{1,0:T(8,128)(2,1)}) fusion(f32[640,3072]{1,0:T(8,128)} %fusion.79, bf16[640,3072]{1,0:T(8,128)(2,1)S(1)} %copy-done.50, f32[640,640]{0,1:T(8,128)S(1)} %get-tuple-element.118, f32[640]{0:T(1024)S(1)} %get-tuple-element.91, f32[640]{0:T(1024)S(1)} %get-tuple-element.130, ...), kind=kOutput, calls=%fused_computation.24 | convolution fusion | flops 2561884160 | bytes 21309440 | tf_op jit(solution)/shard_map/dot_general | solution.py:218
  109.9 3.6 fusion.44
  113.5 2.0 fusion.42
  116.7 1.8 convolution_convert_fusion.12
  118.6 2.6 convolution_convert_fusion.11
  121.3 12.5 %multiply_reduce_fusion.1 = (f32[8,640]{1,0:T(8,128)S(1)}, f32[8,640,640]{1,2,0:T(8,128)}) fusion(f32[8,640,640]{1,2,0:T(8,128)} %copy-done.2, f32[8,640]{1,0:T(8,128)S(1)} %log_add_fusion.1, bf16[640,8,80]{0,2,1:T(8,128)(2,1)S(1)} %bitcast.172, bf16[640,8,80]{0,2,1:T(8,128)(2,1)} %bitcast.186), kind=kOutput, calls=%fused_computation.9 | convolution fusion | flops 534113280 | bytes 27893760 | tf_op jit(solution)/shard_map/qhd,khd->hqk/dot_general | solution.py:121
  133.8 6.6 multiply_convert_fusion.1
  144.1 2.0 convolution_convert_fusion.13
  146.4 3.2 fusion.45
  151.3 1.8 convolution_convert_fusion.14
  153.2 5.6 multiply_convert_fusion.2
  158.8 7.3 fusion.52
  167.0 2.8 fusion.22
  170.1 2.4 convolution_convert_fusion.9
  172.5 12.1 %multiply_reduce_fusion = (f32[8,640]{1,0:T(8,128)S(1)}, f32[8,640,640]{1,2,0:T(8,128)}) fusion(f32[8,640,640]{1,2,0:T(8,128)} %copy-done.1, f32[8,640]{1,0:T(8,128)S(1)} %log_add_fusion, bf16[640,8,80]{0,2,1:T(8,128)(2,1)S(1)} %bitcast.174, bf16[640,8,80]{0,2,1:T(8,128)(2,1)S(1)} %bitcast.184), kind=kOutput, calls=%fused_computation.6 | convolution fusion | flops 534113280 | bytes 27893760 | tf_op jit(solution)/shard_map/qhd,khd->hqk/dot_general | solution.py:121
  185.6 6.6 multiply_convert_fusion
  192.2 2.2 multiply_convert_fusion.3
  195.7 2.2 fusion.55
  198.9 3.9 convolution_convert_fusion.3
  204.0 7.4 %convolution_convert_fusion = bf16[3072,640]{0,1:T(8,128)(2,1)} fusion(bf16[640,640]{0,1:T(8,128)(2,1)S(1)} %copy-done.34, bf16[640,3072]{1,0:T(8,128)(2,1)} %get-tuple-element.120), kind=kOutput, calls=%fused_computation.37 | convolution fusion | flops 2538209280 | bytes 8683520 | tf_op jit(solution)/shard_map/dot_general | solution.py:21
  211.5 8.4 %convolution_convert_fusion.1 = bf16[640,3072]{1,0:T(8,128)(2,1)} fusion(bf16[640,3072]{1,0:T(8,128)(2,1)} %copy-done.55, f32[640,640]{0,1:T(8,128)} %copy-done.18, f32[640]{0:T(1024)S(1)} %get-tuple-element.91, f32[640]{0:T(1024)S(1)} %get-tuple-element.130, f32[640]{0:T(1024)S(1)} %get-tuple-element.108, f32[640]{0:T(1024)S(1)} %get-tuple-element.107), kind=kOutput, calls=%fused_computation.38 | convolution fusion | flops 2520596480 | bytes 9512960 | tf_op jit(solution)/shard_map/dot_general | solution.py:21
  220.7 2.5 copy.170
  223.4 8.2 %reduce-scatter.33.cloned.1.call-done = bf16[3072,320]{0,1:T(8,128)(2,1)} async-done(((bf16[3072,640]{0,1:T(8,128)(2,1)}), bf16[3072,320]{0,1:T(8,128)(2,1)}) %reduce-scatter.33.cloned.1.call-update) | async-done | bytes 1966096 | tf_op jit(solution)/shard_map/reduce_scatter | solution.py:285
  231.6 4.1 copy.180
  235.8 11.1 %reduce-scatter.29.cloned.1.call-done = bf16[640,1536]{1,0:T(8,128)(2,1)} async-done(((bf16[640,3072]{1,0:T(8,128)(2,1)}), bf16[640,1536]{1,0:T(8,128)(2,1)}) %reduce-scatter.29.cloned.1.call-update) | async-done | bytes 1966096 | tf_op jit(solution)/shard_map/reduce_scatter | solution.py:285
  246.9 8.8 %convert_add_fusion.1 = f32[640,640]{0,1:T(8,128)} fusion(f32[640,640]{0,1:T(8,128)} %copy-done.18, bf16[3072,640]{1,0:T(8,128)(2,1)} %param.27, f32[640]{0:T(1024)S(1)} %fusion.61, bf16[640,3072]{1,0:T(8,128)(2,1)} %get-tuple-element.120), kind=kOutput, calls=%fused_computation.93 | convolution fusion | flops 2537881600 | bytes 11143680 | tf_op jit(solution)/shard_map/dot_general | solution.py:221
  255.8 4.8 all-to-all-start.2
  260.6 4.1 convolution_convert_fusion.7
  264.7 4.0 all-to-all-start.5
  268.7 2.9 copy.185
  271.6 4.0 fusion.46
  275.7 3.2 fusion.34
  278.9 4.7 all-to-all-start.4
  286.2 2.7 copy.186
  290.2 40.8 %psum.7 = f32[6,640]{1,0:T(8,128)S(1)} all-reduce(f32[6,640]{1,0:T(8,128)S(1)} %concatenate.13), channel_id=1, replica_groups=mesh['dp'=16,'feat'=2] {'dp','feat'}, use_global_device_ids=true, to_apply=%region_28.29 | all-reduce | flops 3840 | bytes 30720 | tf_op jit(solution)/shard_map/psum | solution.py:270
  331.7 50.3 %all-reduce.7.cloned.1.call-done = (bf16[640,320]{0,1:T(8,128)(2,1)}, bf16[640,320]{0,1:T(8,128)(2,1)}, bf16[640,640]{0,1:T(8,128)(2,1)}, bf16[640,320]{0,1:T(8,128)(2,1)}) async-done(((bf16[640,320]{0,1:T(8,128)(2,1)}, bf16[640,320]{0,1:T(8,128)(2,1)}, bf16[640,640]{0,1:T(8,128)(2,1)}, bf16[640,320]{0,1:T(8,128)(2,1)}), (bf16[640,320]{0,1:T(8,128)(2,1)}, bf16[640,320]{0,1:T(8,128)(2,1)}, ...) | async-done | bytes 2048016
  389.1 73.2 %reduce-scatter.35.cloned.1.call-done = bf16[40,960]{1,0:T(8,128)(2,1)} async-done(((bf16[640,960]{1,0:T(8,128)(2,1)}), bf16[40,960]{1,0:T(8,128)(2,1)}) %reduce-scatter.35.cloned.1.call-update) | async-done | bytes 76816
  464.1 127.7 %reduce-scatter.37.cloned.1.call-done = bf16[192,320]{1,0:T(8,128)(2,1)} async-done(((bf16[3072,320]{1,0:T(8,128)(2,1)}), bf16[192,320]{1,0:T(8,128)(2,1)}) %reduce-scatter.37.cloned.1.call-update) | async-done | bytes 122896
  593.7 129.9 %reduce-scatter.31.cloned.1.call-done = bf16[40,1536]{1,0:T(8,128)(2,1)} async-done(((bf16[640,1536]{1,0:T(8,128)(2,1)}), bf16[40,1536]{1,0:T(8,128)(2,1)}) %reduce-scatter.31.cloned.1.call-update) | async-done | bytes 122896 | tf_op jit(solution)/shard_map/reduce_scatter | solution.py:287
  723.6 1.6 convert_element_type.259
  (221 shorter events, 46.7 us)
Async XLA Ops:
  7.2 40.5 %copy-start = (bf16[640,1920]{1,0:T(8,128)(2,1)S(1)}, bf16[640,1920]{1,0:T(8,128)(2,1)}, u32[]{:S(2)}) copy-start(bf16[640,1920]{1,0:T(8,128)(2,1)} %param.21) | copy-start | bytes 7372804
  7.2 5.8 copy-start.52
  7.2 7.8 %copy-start.53 = (s32[1,24]{1,0:T(1,128)S(1)}, s32[1,24]{1,0:T(1,128)}, u32[]{:S(2)}) copy-start(s32[1,24]{1,0:T(1,128)} %param.18) | copy-start | bytes 292
  7.2 9.3 %copy-start.48 = (f32[3,320]{1,0:T(4,128)S(1)}, f32[3,320]{1,0:T(4,128)}, u32[]{:S(2)}) copy-start(f32[3,320]{1,0:T(4,128)} %param.19) | copy-start | bytes 11524
  7.2 11.3 %copy-start.49 = (f32[3,320]{1,0:T(4,128)S(1)}, f32[3,320]{1,0:T(4,128)}, u32[]{:S(2)}) copy-start(f32[3,320]{1,0:T(4,128)} %param.20) | copy-start | bytes 11524
  9.5 13.7 %all-to-all-start.1 = ((bf16[2,640,320]{1,2,0:T(8,128)(2,1)}), bf16[2,640,320]{1,2,0:T(8,128)(2,1)S(1)}, u32[]{:S(2)}, u32[]{:S(2)}) async-start(bf16[2,640,320]{1,2,0:T(8,128)(2,1)} %bitcast.161), calls=%async_computation.1 | async-start | bytes 1638400 | tf_op jit(solution)/shard_map/all_to_all | solution.py:49
  23.2 4.7 copy-start.29
  23.2 14.9 %all-to-all-start = ((f32[2,640,320]{1,2,0:T(8,128)}), f32[2,640,320]{1,2,0:T(8,128)}, u32[]{:S(2)}, u32[]{:S(2)}) async-start(f32[2,640,320]{1,2,0:T(8,128)} %bitcast.177), calls=%async_computation | async-start | bytes 3276800 | tf_op jit(solution)/shard_map/all_to_all | solution.py:49
  38.0 8.0 %copy-start.42 = (f32[640]{0:T(1024)}, f32[640]{0:T(1024)S(1)}, u32[]{:S(2)}) copy-start(f32[640]{0:T(1024)S(1)} %get-tuple-element.128) | copy-start | bytes 7684
  38.0 19.0 %all-to-all-start.3 = ((f32[2,640,320]{1,2,0:T(8,128)}), f32[2,640,320]{1,2,0:T(8,128)}, u32[]{:S(2)}, u32[]{:S(2)}) async-start(f32[2,640,320]{1,2,0:T(8,128)} %bitcast.176), calls=%async_computation.3 | async-start | bytes 3276800 | tf_op jit(solution)/shard_map/all_to_all | solution.py:49
  42.7 177.3 %reduce-scatter.27.cloned.1.call-start = ((), (), s32[]{:S(2)}) async-start(), calls=%async_computation.20 | async-start | bytes 1228800 | tf_op jit(solution)/shard_map/reduce_scatter | solution.py:285
  45.9 4.0 copy-start.44
  46.0 4.0 copy-start.46
  58.6 8.8 %copy-start.33 = (bf16[640,640]{0,1:T(8,128)(2,1)}, bf16[640,640]{0,1:T(8,128)(2,1)S(1)}, u32[]{:S(2)}) copy-start(bf16[640,640]{0,1:T(8,128)(2,1)S(1)} %fusion.60) | copy-start | bytes 2457604
  58.6 10.0 %copy-start.12 = (bf16[640,640]{0,1:T(8,128)(2,1)S(1)}, bf16[640,640]{0,1:T(8,128)(2,1)}, u32[]{:S(2)}) copy-start(bf16[640,640]{0,1:T(8,128)(2,1)} %copy.140) | copy-start | bytes 2457604
  58.6 10.0 %copy-start.16 = (bf16[640,640]{0,1:T(8,128)(2,1)S(1)}, bf16[640,640]{0,1:T(8,128)(2,1)}, u32[]{:S(2)}) copy-start(bf16[640,640]{0,1:T(8,128)(2,1)} %copy.139) | copy-start | bytes 2457604
  71.1 4.7 copy-start.1
  75.8 3.7 copy-start.20
  83.5 3.2 copy-start.25
  86.7 4.7 copy-start.2
  91.4 3.8 copy-start.9
  91.4 3.8 copy-start.19
  96.4 17.2 %copy-start.18 = (f32[640,640]{0,1:T(8,128)}, f32[640,640]{0,1:T(8,128)S(1)}, u32[]{:S(2)}) copy-start(f32[640,640]{0,1:T(8,128)S(1)} %get-tuple-element.118) | copy-start | bytes 4915204
  109.9 3.6 copy-start.55
  118.6 101.5 %reduce-scatter.23.cloned.1.call-start = ((), (), s32[]{:S(2)}) async-start(), calls=%async_computation.18 | async-start | bytes 1228800 | tf_op jit(solution)/shard_map/reduce_scatter | solution.py:285
  121.2 12.6 %slice-start.4 = ((s8[13107200]{0:T(1024)(128)(4,1)}), s8[4194304]{0:T(1024)(128)(4,1)S(1)}, s32[]{:S(2)}) async-start(s8[13107200]{0:T(1024)(128)(4,1)} %bitcast.164), calls=%async_computation.31 | async-start | bytes 8388608
  121.2 12.5 %slice-start.5 = ((s8[13107200]{0:T(1024)(128)(4,1)}), s8[4194304]{0:T(1024)(128)(4,1)S(1)}, s32[]{:S(2)}) async-start(s8[13107200]{0:T(1024)(128)(4,1)} %bitcast.164), calls=%async_computation.32 | async-start | bytes 8388608
  121.2 12.5 %slice-start.6 = ((s8[13107200]{0:T(1024)(128)(4,1)}), s8[4194304]{0:T(1024)(128)(4,1)S(1)}, s32[]{:S(2)}) async-start(s8[13107200]{0:T(1024)(128)(4,1)} %bitcast.164), calls=%async_computation.33 | async-start | bytes 8388608
  121.2 12.5 %slice-start.7 = ((s8[13107200]{0:T(1024)(128)(4,1)}), s8[524288]{0:T(1024)(128)(4,1)S(1)}, s32[]{:S(2)}) async-start(s8[13107200]{0:T(1024)(128)(4,1)} %bitcast.164), calls=%async_computation.34 | async-start | bytes 1048576
  133.8 6.6 copy-start.15
  140.4 3.7 copy-start.10
  146.1 73.9 %reduce-scatter.21.cloned.1.call-start = ((), (), s32[]{:S(2)}) async-start(), calls=%async_computation.17 | async-start | bytes 1228800 | tf_op jit(solution)/shard_map/reduce_scatter | solution.py:285
  146.3 3.2 copy-start.7
  146.3 3.2 copy-start.11
  153.1 66.9 %reduce-scatter.25.cloned.1.call-start = ((), (), s32[]{:S(2)}) async-start(), calls=%async_computation.19 | async-start | bytes 2457600 | tf_op jit(solution)/shard_map/reduce_scatter | solution.py:285
  158.8 7.3 copy-start.35
  158.8 8.2 %copy-start.30 = (bf16[2,640,320]{1,2,0:T(8,128)(2,1)S(1)}, bf16[2,640,320]{1,2,0:T(8,128)(2,1)}, u32[]{:S(2)}) copy-start(bf16[2,640,320]{1,2,0:T(8,128)(2,1)} %copy-done.29) | copy-start | bytes 2457604
  167.0 3.1 copy-start.21
  169.8 51.0 %reduce-scatter.19.cloned.1.call-start = ((), (), s32[]{:S(2)}) async-start(), calls=%async_computation.16 | async-start | bytes 3686400 | tf_op jit(solution)/shard_map/reduce_scatter | solution.py:285
  172.5 12.1 %slice-start = ((s8[13107200]{0:T(1024)(128)(4,1)}), s8[4194304]{0:T(1024)(128)(4,1)S(1)}, s32[]{:S(2)}) async-start(s8[13107200]{0:T(1024)(128)(4,1)} %bitcast.162), calls=%async_computation.27 | async-start | bytes 8388608
  172.5 12.1 %slice-start.1 = ((s8[13107200]{0:T(1024)(128)(4,1)}), s8[4194304]{0:T(1024)(128)(4,1)S(1)}, s32[]{:S(2)}) async-start(s8[13107200]{0:T(1024)(128)(4,1)} %bitcast.162), calls=%async_computation.28 | async-start | bytes 8388608
  172.5 12.9 %slice-start.2 = ((s8[13107200]{0:T(1024)(128)(4,1)}), s8[4194304]{0:T(1024)(128)(4,1)S(1)}, s32[]{:S(2)}) async-start(s8[13107200]{0:T(1024)(128)(4,1)} %bitcast.162), calls=%async_computation.29 | async-start | bytes 8388608
  172.5 13.1 %slice-start.3 = ((s8[13107200]{0:T(1024)(128)(4,1)}), s8[524288]{0:T(1024)(128)(4,1)S(1)}, s32[]{:S(2)}) async-start(s8[13107200]{0:T(1024)(128)(4,1)} %bitcast.162), calls=%async_computation.30 | async-start | bytes 1048576
  185.6 6.6 copy-start.17
  194.4 3.6 copy-start.38
  195.7 3.2 copy-start.32
  202.8 28.7 %reduce-scatter.33.cloned.1.call-start = ((), (), s32[]{:S(2)}) async-start(), calls=%async_computation.23 | async-start | bytes 5898240 | tf_op jit(solution)/shard_map/reduce_scatter | solution.py:285
  211.4 35.5 %reduce-scatter.29.cloned.1.call-start = ((), (), s32[]{:S(2)}) async-start(), calls=%async_computation.21 | async-start | bytes 5898240 | tf_op jit(solution)/shard_map/reduce_scatter | solution.py:285
  219.9 162.0 %all-reduce.7.cloned.1.call-start = ((), (), s32[]{:S(2)}) async-start(), calls=%async_computation.26 | async-start | bytes 4096000
  220.7 241.6 %reduce-scatter.35.cloned.1.call-start = ((), (), s32[]{:S(2)}) async-start(), calls=%async_computation.24 | async-start | bytes 1392640
  223.3 368.5 %reduce-scatter.37.cloned.1.call-start = ((), (), s32[]{:S(2)}) async-start(), calls=%async_computation.25 | async-start | bytes 2506752
  235.7 487.9 %reduce-scatter.31.cloned.1.call-start = ((), (), s32[]{:S(2)}) async-start(), calls=%async_computation.22 | async-start | bytes 2088960 | tf_op jit(solution)/shard_map/reduce_scatter | solution.py:287
  255.8 4.8 copy-start.36
  255.8 8.9 %all-to-all-start.2 = ((f32[640,2,320]{0,2,1:T(8,128)}), f32[640,2,320]{0,2,1:T(8,128)}, u32[]{:S(2)}, u32[]{:S(2)}) async-start(f32[640,2,320]{0,2,1:T(8,128)} %bitcast.198), calls=%async_computation.2 | async-start | bytes 3276800 | tf_op jit(solution)/shard_map/all_to_all | solution.py:53
  264.6 6.9 copy-start.43
  264.6 6.9 copy-start.45
  264.6 6.9 copy-start.47
  264.7 14.2 %all-to-all-start.5 = ((bf16[640,2,320]{0,2,1:T(8,128)(2,1)}), bf16[640,2,320]{0,2,1:T(8,128)(2,1)S(1)}, u32[]{:S(2)}, u32[]{:S(2)}) async-start(bf16[640,2,320]{0,2,1:T(8,128)(2,1)} %bitcast.202), calls=%async_computation.5 | async-start | bytes 1638400 | tf_op jit(solution)/shard_map/all_to_all | solution.py:53
  268.6 2.9 copy-start.27
  268.6 2.9 copy-start.39
  268.7 2.9 copy-start.41
  271.6 4.1 copy-start.5
  278.9 7.3 all-to-all-start.4
  285.0 4.0 copy-start.54
  (17 other events, 30.8 us)
Sparse Core Ops, SparseCore 0:
  118.7 11.1 reduce-scatter.26
  146.2 11.1 reduce-scatter.22
  159.7 9.4 reduce-scatter.20
  171.9 10.2 reduce-scatter.24
  203.0 13.2 reduce-scatter.18
  218.4 13.0 reduce-scatter.32
  233.8 13.0 reduce-scatter.28
  253.9 128.0 all-reduce.6
  384.2 77.9 reduce-scatter.34
  467.0 124.7 reduce-scatter.36
  597.4 126.1 reduce-scatter.30
where the time goes:
time: 742 us; the launch traced here: 732 us
  waiting for transfers between devices  402 us (54%)
  matrix products  145 us (20%)
  local copies, waits for them, and re-layouts  58 us (8%)
  blocking collectives  44.6 us (6%)
  other arithmetic  38.3 us (5%)
  starting transfers between devices  27.4 us (4%)
  between operations  16.2 us (2%)
    unnamed x14, waiting for transfers between devices  252 us
    reduce_scatter x1, waiting for transfers between devices, per_device(): lax.psum_scatter(pair, 'dp', scatter_dimension=0, tiled=True)  130 us
    psum x1, blocking collectives, per_device(): lax.psum(jnp.concatenate([gain_local, shift_local], axis=0), ('dp', 'feat'))  40.8 us
    unnamed x141, local copies, waits for them, and re-layouts  30 us
    dot_general x7, matrix products, backward_product(): lax.dot_general(grad, weight, (((1,), (1,)), ((), ())), preferred_element...  28.6 us
    dot_general x7, matrix products, inner(): lax.dot_general(left, right, (((0,), (0,)), ((), ())), preferred_element_...  28.2 us
    dot_general x2, matrix products, attend_backward(): jnp.einsum('qhd,khd->hqk', grad_heads, split_heads(values), preferred_ele...  24.6 us
    reduce_scatter x7, waiting for transfers between devices, per_device(): lax.psum_scatter(term.astype(jnp.bfloat16), 'feat', scatter_dimension=1,...  19.4 us
  transfers between devices with their start and end apart: 17, of which 7 were waited for; matrix products, arithmetic and copies ran while one was open for 23% of the time, Pallas kernels for 0%

commit v1 on v0

--- a/solution.py
+++ b/solution.py
@@ -50,7 +50,10 @@
 
 
 def spread_rows(part):
-    return lax.all_to_all(part, "feat", split_axis=1, concat_axis=0, tiled=True)
+    return jnp.concatenate(
+        lax.all_to_all(jnp.stack(jnp.split(part, lax.axis_size("feat"), axis=1)), "feat", 0, 0),
+        axis=0,
+    )
 
 
 def norm_forward(values, gain, shift):

time: 742 us -> 742 us (level)
    reduce_scatter x7, waiting for transfers between devices: 19.4 us -> 10.6 us  [per_device(): lax.psum_scatter(term.astype(jnp.bfloat16), 'feat', scatter_dimension=1,...]
  transfers between devices with their start and end apart: 17 -> 17, of which waited for: 7 -> 7; matrix products, arithmetic and copies ran while one was open for 23% -> 24% of each run, Pallas kernels for 0% -> 0%
where the time goes in v1:
time: 742 us; the launch traced here: 732 us
  waiting for transfers between devices  400 us (54%)
  matrix products  144 us (19%)
  local copies, waits for them, and re-layouts  59.6 us (8%)
  blocking collectives  44.6 us (6%)
  other arithmetic  40.6 us (5%)
  starting transfers between devices  27.3 us (4%)
  between operations  16.2 us (2%)
    unnamed x14, waiting for transfers between devices  258 us
    reduce_scatter x1, waiting for transfers between devices, per_device(): lax.psum_scatter(pair, 'dp', scatter_dimension=0, tiled=True)  130 us
    psum x1, blocking collectives, per_device(): lax.psum(jnp.concatenate([gain_local, shift_local], axis=0), ('dp', 'feat'))  40.8 us
    unnamed x141, local copies, waits for them, and re-layouts  29.9 us
    dot_general x7, matrix products, inner(): lax.dot_general(left, right, (((0,), (0,)), ((), ())), preferred_element_...  28.1 us
    dot_general x7, matrix products, backward_product(): lax.dot_general(grad, weight, (((1,), (1,)), ((), ())), preferred_element...  27.6 us
    dot_general x2, matrix products, attend_backward(): jnp.einsum('qhd,khd->hqk', grad_heads, split_heads(values), preferred_ele...  24.6 us
  transfers between devices with their start and end apart: 17, of which 7 were waited for; matrix products, arithmetic and copies ran while one was open for 24% of the time, Pallas kernels for 0%

profile of v1, /device:TPU:0, one launch (start us, length us, event | category | flops | bytes accessed | tf_op | source)
XLA Modules:
  0.0 732.4 jit_solution(10152509889014786118)
XLA Ops:
  7.2 2.3 copy.190
  9.5 3.5 all-to-all-start.1
  16.5 2.0 all-gather
  18.6 1.8 all-gather.1
  20.5 2.7 copy.189
  23.2 4.7 all-to-all-start
  27.8 2.9 convolution_convert_fusion.6
  31.8 2.2 copy.141
  35.3 2.7 copy.188
  38.0 4.7 all-to-all-start.3
  46.0 1.7 add_convert_fusion.2
  47.7 2.2 convolution_convert_fusion.4
  51.4 2.2 copy.137
  53.5 2.2 copy.136
  58.6 8.8 %fusion.79 = f32[640,3072]{1,0:T(8,128)} fusion(bf16[640,640]{0,1:T(8,128)(2,1)S(1)} %fusion.60, bf16[3072,640]{1,0:T(8,128)(2,1)} %param.27), kind=kOutput, calls=%fused_computation.187 | convolution fusion | flops 2516582400 | bytes 12615680 | tf_op jit(solution)/shard_map/dot_general | solution.py:27
  68.6 2.5 fusion.77
  71.2 1.7 fusion
  72.9 2.9 copy-done.1
  75.8 3.7 fusion.59
  79.6 2.8 fusion.73
  84.2 2.5 fusion.78
  86.7 2.0 fusion.1
  88.7 2.7 copy-done.2
  91.4 3.8 fusion.58
  97.5 12.5 %fusion.7 = (bf16[640,3072]{1,0:T(8,128)(2,1)S(1)}, bf16[640,3072]{1,0:T(8,128)(2,1)}) fusion(f32[640,3072]{1,0:T(8,128)} %fusion.79, bf16[640,3072]{1,0:T(8,128)(2,1)S(1)} %copy-done.50, f32[640,640]{0,1:T(8,128)S(1)} %get-tuple-element.124, f32[640]{0:T(1024)S(1)} %get-tuple-element.91, f32[640]{0:T(1024)S(1)} %get-tuple-element.136, ...), kind=kOutput, calls=%fused_computation.24 | convolution fusion | flops 2561884160 | bytes 21309440 | tf_op jit(solution)/shard_map/dot_general | solution.py:221
  110.0 3.6 fusion.44
  113.6 2.0 fusion.42
  116.7 1.8 convolution_convert_fusion.12
  118.7 2.6 convolution_convert_fusion.11
  121.3 12.5 %multiply_reduce_fusion.1 = (f32[8,640]{1,0:T(8,128)S(1)}, f32[8,640,640]{1,2,0:T(8,128)}) fusion(f32[8,640,640]{1,2,0:T(8,128)} %copy-done.2, f32[8,640]{1,0:T(8,128)S(1)} %log_add_fusion.1, bf16[640,8,80]{0,2,1:T(8,128)(2,1)S(1)} %bitcast.178, bf16[640,8,80]{0,2,1:T(8,128)(2,1)} %bitcast.191), kind=kOutput, calls=%fused_computation.9 | convolution fusion | flops 534113280 | bytes 27893760 | tf_op jit(solution)/shard_map/qhd,khd->hqk/dot_general | solution.py:124
  133.8 6.6 multiply_convert_fusion.1
  144.1 2.0 convolution_convert_fusion.13
  146.3 3.2 fusion.45
  151.3 1.8 convolution_convert_fusion.14
  153.1 5.6 multiply_convert_fusion.2
  158.7 7.3 fusion.52
  166.9 2.8 fusion.22
  170.0 2.4 convolution_convert_fusion.9
  172.5 12.1 %multiply_reduce_fusion = (f32[8,640]{1,0:T(8,128)S(1)}, f32[8,640,640]{1,2,0:T(8,128)}) fusion(f32[8,640,640]{1,2,0:T(8,128)} %copy-done.1, f32[8,640]{1,0:T(8,128)S(1)} %log_add_fusion, bf16[640,8,80]{0,2,1:T(8,128)(2,1)S(1)} %bitcast.180, bf16[640,8,80]{0,2,1:T(8,128)(2,1)S(1)} %bitcast.189), kind=kOutput, calls=%fused_computation.6 | convolution fusion | flops 534113280 | bytes 27893760 | tf_op jit(solution)/shard_map/qhd,khd->hqk/dot_general | solution.py:124
  185.5 6.6 multiply_convert_fusion
  192.1 2.2 multiply_convert_fusion.3
  195.7 2.2 fusion.55
  198.8 3.9 convolution_convert_fusion.3
  203.9 7.4 %convolution_convert_fusion = bf16[3072,640]{0,1:T(8,128)(2,1)} fusion(bf16[640,640]{0,1:T(8,128)(2,1)S(1)} %copy-done.34, bf16[640,3072]{1,0:T(8,128)(2,1)} %get-tuple-element.126), kind=kOutput, calls=%fused_computation.37 | convolution fusion | flops 2538209280 | bytes 8683520 | tf_op jit(solution)/shard_map/dot_general | solution.py:21
  211.4 8.4 %convolution_convert_fusion.1 = bf16[640,3072]{1,0:T(8,128)(2,1)} fusion(bf16[640,3072]{1,0:T(8,128)(2,1)} %copy-done.55, f32[640,640]{0,1:T(8,128)} %copy-done.18, f32[640]{0:T(1024)S(1)} %get-tuple-element.91, f32[640]{0:T(1024)S(1)} %get-tuple-element.136, f32[640]{0:T(1024)S(1)} %get-tuple-element.114, f32[640]{0:T(1024)S(1)} %get-tuple-element.113), kind=kOutput, calls=%fused_computation.38 | convolution fusion | flops 2520596480 | bytes 9512960 | tf_op jit(solution)/shard_map/dot_general | solution.py:21
  220.7 2.5 copy.167
  223.3 8.2 %reduce-scatter.33.cloned.1.call-done = bf16[3072,320]{0,1:T(8,128)(2,1)} async-done(((bf16[3072,640]{0,1:T(8,128)(2,1)}), bf16[3072,320]{0,1:T(8,128)(2,1)}) %reduce-scatter.33.cloned.1.call-update) | async-done | bytes 1966096 | tf_op jit(solution)/shard_map/reduce_scatter | solution.py:288
  231.5 4.1 copy.177
  235.7 8.8 %convert_add_fusion.1 = f32[640,640]{0,1:T(8,128)} fusion(f32[640,640]{0,1:T(8,128)} %copy-done.18, bf16[3072,640]{1,0:T(8,128)(2,1)} %param.27, f32[640]{0:T(1024)S(1)} %fusion.61, bf16[640,3072]{1,0:T(8,128)(2,1)} %get-tuple-element.126), kind=kOutput, calls=%fused_computation.95 | convolution fusion | flops 2537881600 | bytes 11143680 | tf_op jit(solution)/shard_map/dot_general | solution.py:224
  244.5 2.3 reduce-scatter.29.cloned.1.call-done
  249.6 5.1 all-to-all-start.2
  254.7 3.1 convolution_convert_fusion.7
  258.9 3.6 all-to-all-start.5
  262.5 2.9 copy.182
  265.4 4.0 fusion.46
  269.5 2.0 fusion.34
  272.9 4.7 all-to-all-start.4
  280.2 2.7 copy.183
  284.2 40.8 %psum.7 = f32[6,640]{1,0:T(8,128)S(1)} all-reduce(f32[6,640]{1,0:T(8,128)S(1)} %concatenate.13), channel_id=1, replica_groups=mesh['dp'=16,'feat'=2] {'dp','feat'}, use_global_device_ids=true, to_apply=%region_28.29 | all-reduce | flops 3840 | bytes 30720 | tf_op jit(solution)/shard_map/psum | solution.py:273
  325.7 56.5 %all-reduce.7.cloned.1.call-done = (bf16[640,320]{0,1:T(8,128)(2,1)}, bf16[640,320]{0,1:T(8,128)(2,1)}, bf16[640,640]{0,1:T(8,128)(2,1)}, bf16[640,320]{0,1:T(8,128)(2,1)}) async-done(((bf16[640,320]{0,1:T(8,128)(2,1)}, bf16[640,320]{0,1:T(8,128)(2,1)}, bf16[640,640]{0,1:T(8,128)(2,1)}, bf16[640,320]{0,1:T(8,128)(2,1)}), (bf16[640,320]{0,1:T(8,128)(2,1)}, bf16[640,320]{0,1:T(8,128)(2,1)}, ...) | async-done | bytes 2048016
  389.3 73.2 %reduce-scatter.35.cloned.1.call-done = bf16[40,960]{1,0:T(8,128)(2,1)} async-done(((bf16[640,960]{1,0:T(8,128)(2,1)}), bf16[40,960]{1,0:T(8,128)(2,1)}) %reduce-scatter.35.cloned.1.call-update) | async-done | bytes 76816
  464.3 127.7 %reduce-scatter.37.cloned.1.call-done = bf16[192,320]{1,0:T(8,128)(2,1)} async-done(((bf16[3072,320]{1,0:T(8,128)(2,1)}), bf16[192,320]{1,0:T(8,128)(2,1)}) %reduce-scatter.37.cloned.1.call-update) | async-done | bytes 122896
  593.9 129.9 %reduce-scatter.31.cloned.1.call-done = bf16[40,1536]{1,0:T(8,128)(2,1)} async-done(((bf16[640,1536]{1,0:T(8,128)(2,1)}), bf16[40,1536]{1,0:T(8,128)(2,1)}) %reduce-scatter.31.cloned.1.call-update) | async-done | bytes 122896 | tf_op jit(solution)/shard_map/reduce_scatter | solution.py:290
  723.8 1.6 convert_element_type.255
  (227 shorter events, 51.9 us)
Async XLA Ops:
  7.2 40.5 %copy-start = (bf16[640,1920]{1,0:T(8,128)(2,1)S(1)}, bf16[640,1920]{1,0:T(8,128)(2,1)}, u32[]{:S(2)}) copy-start(bf16[640,1920]{1,0:T(8,128)(2,1)} %param.21) | copy-start | bytes 7372804
  7.2 5.8 copy-start.52
  7.2 7.8 %copy-start.53 = (s32[1,24]{1,0:T(1,128)S(1)}, s32[1,24]{1,0:T(1,128)}, u32[]{:S(2)}) copy-start(s32[1,24]{1,0:T(1,128)} %param.18) | copy-start | bytes 292
  7.2 9.3 %copy-start.48 = (f32[3,320]{1,0:T(4,128)S(1)}, f32[3,320]{1,0:T(4,128)}, u32[]{:S(2)}) copy-start(f32[3,320]{1,0:T(4,128)} %param.19) | copy-start | bytes 11524
  7.2 11.3 %copy-start.49 = (f32[3,320]{1,0:T(4,128)S(1)}, f32[3,320]{1,0:T(4,128)}, u32[]{:S(2)}) copy-start(f32[3,320]{1,0:T(4,128)} %param.20) | copy-start | bytes 11524
  9.5 13.7 %all-to-all-start.1 = ((bf16[2,640,320]{1,2,0:T(8,128)(2,1)}), bf16[2,640,320]{1,2,0:T(8,128)(2,1)S(1)}, u32[]{:S(2)}, u32[]{:S(2)}) async-start(bf16[2,640,320]{1,2,0:T(8,128)(2,1)} %bitcast.167), calls=%async_computation.1 | async-start | bytes 1638400 | tf_op jit(solution)/shard_map/all_to_all | solution.py:49
  23.2 4.7 copy-start.29
  23.2 14.9 %all-to-all-start = ((f32[2,640,320]{1,2,0:T(8,128)}), f32[2,640,320]{1,2,0:T(8,128)}, u32[]{:S(2)}, u32[]{:S(2)}) async-start(f32[2,640,320]{1,2,0:T(8,128)} %bitcast.183), calls=%async_computation | async-start | bytes 3276800 | tf_op jit(solution)/shard_map/all_to_all | solution.py:49
  38.0 8.0 %copy-start.42 = (f32[640]{0:T(1024)}, f32[640]{0:T(1024)S(1)}, u32[]{:S(2)}) copy-start(f32[640]{0:T(1024)S(1)} %get-tuple-element.134) | copy-start | bytes 7684
  38.0 19.0 %all-to-all-start.3 = ((f32[2,640,320]{1,2,0:T(8,128)}), f32[2,640,320]{1,2,0:T(8,128)}, u32[]{:S(2)}, u32[]{:S(2)}) async-start(f32[2,640,320]{1,2,0:T(8,128)} %bitcast.182), calls=%async_computation.3 | async-start | bytes 3276800 | tf_op jit(solution)/shard_map/all_to_all | solution.py:49
  42.7 177.2 %reduce-scatter.27.cloned.1.call-start = ((), (), s32[]{:S(2)}) async-start(), calls=%async_computation.20 | async-start | bytes 1228800 | tf_op jit(solution)/shard_map/reduce_scatter | solution.py:288
  45.9 4.0 copy-start.44
  46.0 4.0 copy-start.46
  58.6 8.8 %copy-start.33 = (bf16[640,640]{0,1:T(8,128)(2,1)}, bf16[640,640]{0,1:T(8,128)(2,1)S(1)}, u32[]{:S(2)}) copy-start(bf16[640,640]{0,1:T(8,128)(2,1)S(1)} %fusion.60) | copy-start | bytes 2457604
  58.6 10.0 %copy-start.12 = (bf16[640,640]{0,1:T(8,128)(2,1)S(1)}, bf16[640,640]{0,1:T(8,128)(2,1)}, u32[]{:S(2)}) copy-start(bf16[640,640]{0,1:T(8,128)(2,1)} %copy.137) | copy-start | bytes 2457604
  58.6 10.0 %copy-start.16 = (bf16[640,640]{0,1:T(8,128)(2,1)S(1)}, bf16[640,640]{0,1:T(8,128)(2,1)}, u32[]{:S(2)}) copy-start(bf16[640,640]{0,1:T(8,128)(2,1)} %copy.136) | copy-start | bytes 2457604
  71.1 4.7 copy-start.1
  75.8 3.7 copy-start.20
  83.6 3.1 copy-start.25
  86.7 4.7 copy-start.2
  91.4 3.8 copy-start.9
  91.4 3.8 copy-start.19
  96.4 17.2 %copy-start.18 = (f32[640,640]{0,1:T(8,128)}, f32[640,640]{0,1:T(8,128)S(1)}, u32[]{:S(2)}) copy-start(f32[640,640]{0,1:T(8,128)S(1)} %get-tuple-element.124) | copy-start | bytes 4915204
  109.9 3.6 copy-start.55
  118.6 101.4 %reduce-scatter.23.cloned.1.call-start = ((), (), s32[]{:S(2)}) async-start(), calls=%async_computation.18 | async-start | bytes 1228800 | tf_op jit(solution)/shard_map/reduce_scatter | solution.py:288
  121.2 12.6 %slice-start.4 = ((s8[13107200]{0:T(1024)(128)(4,1)}), s8[4194304]{0:T(1024)(128)(4,1)S(1)}, s32[]{:S(2)}) async-start(s8[13107200]{0:T(1024)(128)(4,1)} %bitcast.170), calls=%async_computation.31 | async-start | bytes 8388608
  121.3 12.6 %slice-start.5 = ((s8[13107200]{0:T(1024)(128)(4,1)}), s8[4194304]{0:T(1024)(128)(4,1)S(1)}, s32[]{:S(2)}) async-start(s8[13107200]{0:T(1024)(128)(4,1)} %bitcast.170), calls=%async_computation.32 | async-start | bytes 8388608
  121.3 12.5 %slice-start.6 = ((s8[13107200]{0:T(1024)(128)(4,1)}), s8[4194304]{0:T(1024)(128)(4,1)S(1)}, s32[]{:S(2)}) async-start(s8[13107200]{0:T(1024)(128)(4,1)} %bitcast.170), calls=%async_computation.33 | async-start | bytes 8388608
  121.3 12.5 %slice-start.7 = ((s8[13107200]{0:T(1024)(128)(4,1)}), s8[524288]{0:T(1024)(128)(4,1)S(1)}, s32[]{:S(2)}) async-start(s8[13107200]{0:T(1024)(128)(4,1)} %bitcast.170), calls=%async_computation.34 | async-start | bytes 1048576
  133.8 6.6 copy-start.15
  140.5 3.6 copy-start.10
  146.1 73.9 %reduce-scatter.21.cloned.1.call-start = ((), (), s32[]{:S(2)}) async-start(), calls=%async_computation.17 | async-start | bytes 1228800 | tf_op jit(solution)/shard_map/reduce_scatter | solution.py:288
  146.3 3.2 copy-start.7
  146.3 3.2 copy-start.11
  153.1 66.9 %reduce-scatter.25.cloned.1.call-start = ((), (), s32[]{:S(2)}) async-start(), calls=%async_computation.19 | async-start | bytes 2457600 | tf_op jit(solution)/shard_map/reduce_scatter | solution.py:288
  158.7 7.3 copy-start.37
  158.7 8.2 %copy-start.30 = (bf16[2,640,320]{1,2,0:T(8,128)(2,1)S(1)}, bf16[2,640,320]{1,2,0:T(8,128)(2,1)}, u32[]{:S(2)}) copy-start(bf16[2,640,320]{1,2,0:T(8,128)(2,1)} %copy-done.29) | copy-start | bytes 2457604
  166.9 3.1 copy-start.21
  169.7 50.9 %reduce-scatter.19.cloned.1.call-start = ((), (), s32[]{:S(2)}) async-start(), calls=%async_computation.16 | async-start | bytes 3686400 | tf_op jit(solution)/shard_map/reduce_scatter | solution.py:288
  172.4 12.1 %slice-start = ((s8[13107200]{0:T(1024)(128)(4,1)}), s8[4194304]{0:T(1024)(128)(4,1)S(1)}, s32[]{:S(2)}) async-start(s8[13107200]{0:T(1024)(128)(4,1)} %bitcast.168), calls=%async_computation.27 | async-start | bytes 8388608
  172.4 12.1 %slice-start.1 = ((s8[13107200]{0:T(1024)(128)(4,1)}), s8[4194304]{0:T(1024)(128)(4,1)S(1)}, s32[]{:S(2)}) async-start(s8[13107200]{0:T(1024)(128)(4,1)} %bitcast.168), calls=%async_computation.28 | async-start | bytes 8388608
  172.5 12.9 %slice-start.2 = ((s8[13107200]{0:T(1024)(128)(4,1)}), s8[4194304]{0:T(1024)(128)(4,1)S(1)}, s32[]{:S(2)}) async-start(s8[13107200]{0:T(1024)(128)(4,1)} %bitcast.168), calls=%async_computation.29 | async-start | bytes 8388608
  172.5 13.1 %slice-start.3 = ((s8[13107200]{0:T(1024)(128)(4,1)}), s8[524288]{0:T(1024)(128)(4,1)S(1)}, s32[]{:S(2)}) async-start(s8[13107200]{0:T(1024)(128)(4,1)} %bitcast.168), calls=%async_computation.30 | async-start | bytes 1048576
  185.5 6.6 copy-start.17
  194.3 3.6 copy-start.35
  195.7 3.2 copy-start.32
  202.8 28.7 %reduce-scatter.33.cloned.1.call-start = ((), (), s32[]{:S(2)}) async-start(), calls=%async_computation.23 | async-start | bytes 5898240 | tf_op jit(solution)/shard_map/reduce_scatter | solution.py:288
  211.3 35.5 %reduce-scatter.29.cloned.1.call-start = ((), (), s32[]{:S(2)}) async-start(), calls=%async_computation.21 | async-start | bytes 5898240 | tf_op jit(solution)/shard_map/reduce_scatter | solution.py:288
  219.8 162.3 %all-reduce.7.cloned.1.call-start = ((), (), s32[]{:S(2)}) async-start(), calls=%async_computation.26 | async-start | bytes 4096000
  220.6 241.9 %reduce-scatter.35.cloned.1.call-start = ((), (), s32[]{:S(2)}) async-start(), calls=%async_computation.24 | async-start | bytes 1392640
  223.2 368.8 %reduce-scatter.37.cloned.1.call-start = ((), (), s32[]{:S(2)}) async-start(), calls=%async_computation.25 | async-start | bytes 2506752
  235.6 488.2 %reduce-scatter.31.cloned.1.call-start = ((), (), s32[]{:S(2)}) async-start(), calls=%async_computation.22 | async-start | bytes 2088960 | tf_op jit(solution)/shard_map/reduce_scatter | solution.py:290
  249.6 5.1 copy-start.38
  249.6 9.3 %all-to-all-start.2 = ((f32[2,640,320]{1,2,0:T(8,128)}), f32[2,640,320]{1,2,0:T(8,128)}, u32[]{:S(2)}, u32[]{:S(2)}) async-start(f32[2,640,320]{1,2,0:T(8,128)} %pad_maximum_fusion.1), calls=%async_computation.2 | async-start | bytes 3276800 | tf_op jit(solution)/shard_map/all_to_all | solution.py:54
  258.9 14.0 %all-to-all-start.5 = ((bf16[2,640,320]{1,2,0:T(8,128)(2,1)}), bf16[2,640,320]{1,2,0:T(8,128)(2,1)S(1)}, u32[]{:S(2)}, u32[]{:S(2)}) async-start(bf16[2,640,320]{1,2,0:T(8,128)(2,1)} %pad_maximum_fusion.8), calls=%async_computation.5 | async-start | bytes 1638400 | tf_op jit(solution)/shard_map/all_to_all | solution.py:54
  262.4 2.9 copy-start.27
  262.4 2.9 copy-start.36
  262.4 2.9 copy-start.41
  262.5 2.9 copy-start.43
  262.5 2.9 copy-start.45
  262.5 2.9 copy-start.47
  265.4 4.1 copy-start.5
  272.9 7.3 all-to-all-start.4
  279.0 4.0 copy-start.54
  (17 other events, 30.7 us)
Sparse Core Ops, SparseCore 0:
  118.7 11.1 reduce-scatter.26
  146.2 11.1 reduce-scatter.22
  159.7 9.4 reduce-scatter.20
  171.9 10.2 reduce-scatter.24
  202.9 13.2 reduce-scatter.18
  218.4 13.0 reduce-scatter.32
  233.7 13.0 reduce-scatter.28
  253.8 128.3 all-reduce.6
  384.5 77.9 reduce-scatter.34
  467.2 124.7 reduce-scatter.36
  597.7 126.0 reduce-scatter.30
